TPU v7x, 512 devices: a whole 4x4x16 slice. The times are simulated.
512 devices in a mesh: dp: 32 (over z_lo, x, core), mp: 16 (over z_hi, y).
Axes of the slice: x: 4, y: 4, z: 16 (z_hi: 4, z_lo: 4; z = z_hi * 4 + z_lo), core: 2. Of those that a mesh axis runs over, the one named last changes fastest.
Arguments:
- grads: bfloat16 [32, 2, 256, 28672], P('dp', None, None, 'mp'), may hold values from -6 to 6
- weights: bfloat16 [2, 256, 28672], P(None, 'dp', 'mp'), may hold values from -1.5 to 1.5
- first_moment: float32 [2, 256, 256], P(None, 'dp'), may hold values from -6 to 6
- second_moment: float32 [2, 256, 256], P(None, 'dp'), may hold values from 1 to 16
- old_seeds: int32 [2], replicated, may hold values from 0 to 999999
- new_seeds: int32 [2], replicated, may hold values from 0 to 999999
Outputs:
- new_weights: bfloat16 [2, 256, 28672], P(None, None, 'mp')
- new_first: float32 [2, 256, 256], P(None, 'dp')
- new_second: float32 [2, 256, 256], P(None, 'dp')
Inputs may be any that keep to these rules, and one draw needn't show every extreme that they name: `old_seeds`: seeds of the counter-based generator; old and new seeds are drawn independently. `new_seeds`: seeds of the counter-based generator; old and new seeds are drawn independently.
All inputs are finite; a program needn't handle non-finite values.
Results may differ from a plain program's by a relative error of at most 0.0053.
Values may be sent and summed in bfloat16 or wider, within the bound.
No kernel may reach another device: no remote copies, remote signals or barrier semaphores. Data moves between devices by JAX's collectives and lax.ppermute only.
A program may use at most 64 MiB of HBM per device.

v0:
```python
import math
import jax
import jax.numpy as jnp
from jax import lax
from jax.sharding import PartitionSpec as P


def scramble(values):
    return (values % 46000 * (values // 2 % 46000 + 1) + 12345) % 65521


def generate(seed_value, rank_ids, columns):
    offset = seed_value % 65521
    row_key = (rank_ids * 251 + offset * 3) % 65521
    col_key = scramble((columns * 7 + offset) % 65521)
    hashed = scramble((row_key[:, None] + 2 * col_key[None, :]) % 65521)
    hashed = scramble((hashed * 3 + row_key[:, None]) % 65521)
    spread = math.sqrt(12.0 / rank_ids.shape[0])
    return ((hashed.astype(jnp.float32) + 0.5) / 65521.0 - 0.5) * spread


def inner_rank(left, right):
    return lax.dot_general(
        left, right, (((1,), (1,)), ((), ())), preferred_element_type=jnp.float32
    )


def shards(grads, weights, first_moment, second_moment, old_seeds, new_seeds):
    layers = weights.shape[0]
    rank = first_moment.shape[2]
    ncols = weights.shape[2]
    col_start = lax.axis_index("mp") * ncols
    columns = col_start + jnp.arange(ncols, dtype=jnp.int32)
    rank_ids = jnp.arange(rank, dtype=jnp.int32)
    new_projs = [
        generate(new_seeds[layer_id], rank_ids, columns).astype(jnp.bfloat16)
        for layer_id in range(layers)
    ]
    gathered = []
    firsts = []
    seconds = []
    for layer_id in range(layers):
        new_proj = new_projs[layer_id]
        old_proj = generate(old_seeds[layer_id], rank_ids, columns).astype(jnp.bfloat16)
        gram_matrix = lax.psum(inner_rank(old_proj, new_proj), "mp")
        partial_value = inner_rank(grads[0, layer_id], new_proj)
        owned = lax.psum_scatter(partial_value, "dp", scatter_dimension=0, tiled=True)
        compressed = lax.psum(owned, "mp")
        moment = (
            0.9 * jnp.dot(first_moment[layer_id], gram_matrix, precision=lax.Precision.HIGHEST)
            + 0.1 * compressed
        )
        second = (
            0.95
            * jnp.dot(
                second_moment[layer_id], gram_matrix * gram_matrix, precision=lax.Precision.HIGHEST
            )
            + 0.05 * compressed * compressed
        )
        direction = (moment / (jnp.sqrt(second) + 1e-08)).astype(jnp.bfloat16)
        update = jnp.dot(direction, new_proj, preferred_element_type=jnp.float32)
        block = (weights[layer_id].astype(jnp.float32) - 0.5 * update).astype(jnp.bfloat16)
        gathered.append(lax.all_gather(block, "dp", axis=0, tiled=True))
        firsts.append(moment)
        seconds.append(second)
    new_weights = jnp.stack(gathered)
    return (new_weights, jnp.stack(firsts), jnp.stack(seconds))


def solution(mesh):
    placed = (
        P("dp", None, None, "mp"),
        P(None, "dp", "mp"),
        P(None, "dp", None),
        P(None, "dp", None),
        P(),
        P(),
    )
    return jax.shard_map(
        shards,
        mesh=mesh,
        in_specs=placed,
        out_specs=(P(None, None, "mp"), P(None, "dp", None), P(None, "dp", None)),
        check_vma=False,
    )
```

profile of v0, /device:TPU:1, one launch (start us, length us, event | category | flops | bytes accessed | tf_op | source)
XLA Modules:
  0.0 542.0 jit_solution(2791521066732754462)
XLA Ops:
  8.0 0.0 reduce-scatter.5.cloned.1.call-start
  8.0 1.3 fusion.313
  10.1 0.0 copy-start.3
  10.1 11.9 %convolution_bitcast_fusion = f32[256,256]{1,0:T(8,128)} fusion(bf16[1,2,256,1792]{3,2,1,0:T(8,128)(2,1)} %param.6, s32[1792]{0:T(1024)S(1)} %fusion.205, s32[256]{0:T(256)S(1)} %and_select_fusion), kind=kOutput, calls=%fused_computation.211 | convolution fusion | flops 277544960 | bytes 1187840 | tf_op jit(solution)/shard_map/dot_general | solution.py:23
  22.0 0.0 reduce-scatter.5.cloned.1.call-update
  22.1 0.3 reduce-scatter.3.cloned.1.call-start
  23.1 0.0 copy-done.3
  23.1 0.0 copy-start.2
  23.1 10.6 %convolution_bitcast_fusion.1 = f32[256,256]{1,0:T(8,128)} fusion(bf16[1,2,256,1792]{3,2,1,0:T(8,128)(2,1)S(1)} %copy-done.3, s32[1792]{0:T(1024)S(1)} %fusion.191, s32[256]{0:T(256)S(1)} %and_select_fusion.2), kind=kOutput, calls=%fused_computation.212 | convolution fusion | flops 277544960 | bytes 1188864 | tf_op jit(solution)/shard_map/dot_general | solution.py:23
  33.7 0.0 reduce-scatter.3.cloned.1.call-update
  33.8 0.4 all-reduce.4.cloned.1.call-start
  34.2 0.0 copy-done.2
  34.2 0.6 fusion.312
  36.1 0.1 fusion.184
  36.2 20.4 %fusion.138 = f32[256,256]{1,0:T(8,128)} fusion(s32[1792]{0:T(1024)S(1)} %fusion.191, s32[256]{0:T(256)S(1)} %and_select_fusion.2, s32[1792]{0:T(1024)S(1)} %get-tuple-element.11, s32[256]{0:T(256)S(1)} %and_select_fusion.3), kind=kOutput, calls=%fused_computation.226 | convolution fusion | flops 320208896 | bytes 278528 | tf_op jit(solution)/shard_map/dot_general | solution.py:23
  56.7 0.0 copy-start
  56.7 0.0 copy-start.1
  56.7 0.0 copy-start.4
  56.7 20.8 %fusion.136 = f32[256,256]{1,0:T(8,128)} fusion(s32[1792]{0:T(1024)S(1)} %get-tuple-element.12, s32[256]{0:T(256)S(1)} %and_select_fusion.1, s32[1792]{0:T(1024)S(1)} %fusion.205, s32[256]{0:T(256)S(1)} %and_select_fusion), kind=kOutput, calls=%fused_computation.225 | convolution fusion | flops 320208896 | bytes 278528 | tf_op jit(solution)/shard_map/dot_general | solution.py:23
  77.5 0.0 all-reduce.4.cloned.1.call-update
  77.5 95.8 %reduce-scatter.5.cloned.1.call-done = f32[8,256]{1,0:T(8,128)} async-done(((f32[256,256]{1,0:T(8,128)}), f32[8,256]{1,0:T(8,128)}) %reduce-scatter.5.cloned.1.call-update) | async-done | bytes 8208 | tf_op jit(solution)/shard_map/reduce_scatter | solution.py:47
  173.4 149.7 %reduce-scatter.3.cloned.1.call-done = f32[8,256]{1,0:T(8,128)} async-done(((f32[256,256]{1,0:T(8,128)}), f32[8,256]{1,0:T(8,128)}) %reduce-scatter.3.cloned.1.call-update) | async-done | bytes 8208 | tf_op jit(solution)/shard_map/reduce_scatter | solution.py:47
  323.1 84.7 %all-reduce = (f32[8,256]{1,0:T(8,128)S(1)}, f32[8,256]{1,0:T(8,128)S(1)}) all-reduce(f32[8,256]{1,0:T(8,128)} %reduce-scatter.5.cloned.1.call-done, f32[8,256]{1,0:T(8,128)} %reduce-scatter.3.cloned.1.call-done), channel_id=1, replica_groups=mesh['dp'=32,'mp'=16] {'mp'}, use_global_device_ids=true, to_apply=%region_5.6 | all-reduce | flops 4096 | bytes 32768 | tf_op jit(solution)/shard_map/psum | solution.py:48
  407.8 0.0 all-reduce.4.cloned.1.call-done
  407.8 0.0 copy-done
  407.8 1.2 fusion.129
  408.9 0.0 copy-done.1
  409.0 1.2 fusion.131
  410.1 1.2 fusion.133
  411.4 1.2 fusion.135
  412.6 0.0 copy-done.4
  412.6 9.8 %fusion.3 = bf16[8,1792]{1,0:T(8,128)(2,1)S(1)} fusion(s32[1792]{0:T(1024)S(1)} %fusion.205, s32[256]{0:T(256)S(1)} %and_select_fusion, bf16[2,8,1792]{2,1,0:T(8,128)(2,1)S(1)} %copy-done.4, f32[8,256]{1,0:T(8,128)S(1)} %fusion.131, f32[8,256]{1,0:T(8,128)S(1)} %fusion.129), kind=kOutput, calls=%fused_computation.69 | convolution fusion | flops 50067456 | bytes 81920 | tf_op jit(solution)/shard_map/dot_general | solution.py:61
  422.4 57.5 %all_gather.7 = bf16[256,1792]{1,0:T(8,128)(2,1)S(1)} all-gather(bf16[8,1792]{1,0:T(8,128)(2,1)S(1)} %fusion.3), channel_id=1, replica_groups=mesh['dp'=32,'mp'=16] {'dp'}, dimensions={0}, use_global_device_ids=true | all-gather | bytes 946176 | tf_op jit(solution)/shard_map/all_gather | solution.py:63
  479.9 9.8 %fusion.2 = bf16[8,1792]{1,0:T(8,128)(2,1)S(1)} fusion(s32[1792]{0:T(1024)S(1)} %fusion.191, s32[256]{0:T(256)S(1)} %and_select_fusion.2, bf16[2,8,1792]{2,1,0:T(8,128)(2,1)S(1)} %copy-done.4, f32[8,256]{1,0:T(8,128)S(1)} %fusion.135, f32[8,256]{1,0:T(8,128)S(1)} %fusion.133), kind=kOutput, calls=%fused_computation.68 | convolution fusion | flops 50067456 | bytes 81920 | tf_op jit(solution)/shard_map/dot_general | solution.py:61
  489.7 41.9 %all_gather.6 = bf16[256,1792]{1,0:T(8,128)(2,1)S(1)} all-gather(bf16[8,1792]{1,0:T(8,128)(2,1)S(1)} %fusion.2), channel_id=1, replica_groups=mesh['dp'=32,'mp'=16] {'dp'}, dimensions={0}, use_global_device_ids=true | all-gather | bytes 946176 | tf_op jit(solution)/shard_map/all_gather | solution.py:63
  531.6 0.6 pad_maximum_fusion.2
  532.2 0.6 pad_maximum_fusion.1
  532.8 1.4 pad_maximum_fusion
  (6 shorter events, 0.2 us)
Async XLA Ops:
  8.0 165.4 %reduce-scatter.5.cloned.1.call-start = ((), (), s32[]{:S(2)}) async-start(), calls=%async_computation.3 | async-start | bytes 270336 | tf_op jit(solution)/shard_map/reduce_scatter | solution.py:47
  10.1 13.0 %copy-start.3 = (bf16[1,2,256,1792]{3,2,1,0:T(8,128)(2,1)S(1)}, bf16[1,2,256,1792]{3,2,1,0:T(8,128)(2,1)}, u32[]{:S(2)}) copy-start(bf16[1,2,256,1792]{3,2,1,0:T(8,128)(2,1)} %param.6) | copy-start | bytes 5505028
  22.1 301.0 %reduce-scatter.3.cloned.1.call-start = ((), (), s32[]{:S(2)}) async-start(), calls=%async_computation.2 | async-start | bytes 270336 | tf_op jit(solution)/shard_map/reduce_scatter | solution.py:47
  23.1 11.1 %copy-start.2 = (s32[2]{0:T(128)S(1)}, s32[2]{0:T(128)}, u32[]{:S(2)}) copy-start(s32[2]{0:T(128)} %param.10) | copy-start | bytes 28
  33.8 374.0 %all-reduce.4.cloned.1.call-start = ((), (), s32[]{:S(2)}) async-start(), calls=%async_computation.4 | async-start | bytes 1048576 | tf_op jit(solution)/shard_map/psum | solution.py:45
  56.7 351.1 %copy-start = (f32[2,8,256]{2,1,0:T(8,128)S(1)}, f32[2,8,256]{2,1,0:T(8,128)}, u32[]{:S(2)}) copy-start(f32[2,8,256]{2,1,0:T(8,128)} %param.9) | copy-start | bytes 49156
  56.7 352.3 %copy-start.1 = (f32[2,8,256]{2,1,0:T(8,128)S(1)}, f32[2,8,256]{2,1,0:T(8,128)}, u32[]{:S(2)}) copy-start(f32[2,8,256]{2,1,0:T(8,128)} %param.8) | copy-start | bytes 49156
  56.7 355.9 %copy-start.4 = (bf16[2,8,1792]{2,1,0:T(8,128)(2,1)S(1)}, bf16[2,8,1792]{2,1,0:T(8,128)(2,1)}, u32[]{:S(2)}) copy-start(bf16[2,8,1792]{2,1,0:T(8,128)(2,1)} %param.7) | copy-start | bytes 172036
Sparse Core Ops, SparseCore 0:
  22.2 151.1 reduce-scatter.4
  176.1 146.8 reduce-scatter.2
Sparse Core Ops, SparseCore 1:
  77.6 199.6 all-reduce.3
where the time goes:
time: 550 us; the launch traced here: 542 us
  waiting for transfers between devices  246 us (45%)
  blocking collectives  184 us (33%)
  matrix products  88.2 us (16%)
  between operations  18.6 us (3%)
    reduce_scatter x2, waiting for transfers between devices, shards(): lax.psum_scatter(partial_value, 'dp', scatter_dimension=0, tiled=True)  246 us
    all_gather x2, blocking collectives, shards(): gathered.append(lax.all_gather(block, 'dp', axis=0, tiled=True))  99.4 us
    psum x1, blocking collectives, shards(): compressed = lax.psum(owned, 'mp')  84.7 us
    dot_general x4, matrix products, inner_rank(): lax.dot_general(left, right, (((1,), (1,)), ((), ())), preferred_element_...  63.8 us
    dot_general x2, matrix products, shards(): update = jnp.dot(direction, new_proj, preferred_element_type=jnp.float32)  19.6 us
  transfers between devices with their start and end apart: 3, of which 2 were waited for; matrix products, arithmetic and copies ran while one was open for 10% of the time, Pallas kernels for 0%

commit v1 on v0

--- a/solution.py
+++ b/solution.py
@@ -60,7 +60,17 @@
         direction = (moment / (jnp.sqrt(second) + 1e-08)).astype(jnp.bfloat16)
         update = jnp.dot(direction, new_proj, preferred_element_type=jnp.float32)
         block = (weights[layer_id].astype(jnp.float32) - 0.5 * update).astype(jnp.bfloat16)
-        gathered.append(lax.all_gather(block, "dp", axis=0, tiled=True))
+        gathered.append(
+            jnp.concatenate(
+                lax.all_to_all(
+                    jnp.stack([block] * lax.psum(1, axis_name="dp")),
+                    axis_name="dp",
+                    split_axis=0,
+                    concat_axis=0,
+                ),
+                axis=0,
+            )
+        )
         firsts.append(moment)
         seconds.append(second)
     new_weights = jnp.stack(gathered)

time: 550 us -> 513 us (0.933)
  blocking collectives: 184 us -> 84.4 us
  waiting for transfers between devices: 246 us -> 282 us
  starting transfers between devices: 0.74 us -> 26.6 us
    all_gather x2 -> x0, blocking collectives: 99.4 us -> none  [shards(): gathered.append(lax.all_gather(block, 'dp', axis=0, tiled=True))]
    all_to_all x0 -> x2, waiting for transfers between devices: none -> 36.5 us  [shards(): lax.all_to_all(jnp.stack([block] * lax.psum(1, axis_name='dp')), axis_nam...]
    all_to_all x0 -> x2, starting transfers between devices: none -> 25.9 us  [shards(): lax.all_to_all(jnp.stack([block] * lax.psum(1, axis_name='dp')), axis_nam...]
  transfers between devices with their start and end apart: 3 -> 5, of which waited for: 2 -> 4; matrix products, arithmetic and copies ran while one was open for 10% -> 13% of each run, Pallas kernels for 0% -> 0%
where the time goes in v1:
time: 513 us; the launch traced here: 505 us
  waiting for transfers between devices  282 us (55%)
  matrix products  86.3 us (17%)
  blocking collectives  84.4 us (16%)
  starting transfers between devices  26.6 us (5%)
  between operations  18.6 us (4%)
    reduce_scatter x2, waiting for transfers between devices, shards(): lax.psum_scatter(partial_value, 'dp', scatter_dimension=0, tiled=True)  246 us
    psum x1, blocking collectives, shards(): compressed = lax.psum(owned, 'mp')  84.4 us
    dot_general x4, matrix products, inner_rank(): lax.dot_general(left, right, (((1,), (1,)), ((), ())), preferred_element_...  63.8 us
    all_to_all x2, waiting for transfers between devices, shards(): lax.all_to_all(jnp.stack([block] * lax.psum(1, axis_name='dp')), axis_nam...  36.5 us
    all_to_all x2, starting transfers between devices, shards(): lax.all_to_all(jnp.stack([block] * lax.psum(1, axis_name='dp')), axis_nam...  25.9 us
    dot_general x2, matrix products, shards(): update = jnp.dot(direction, new_proj, preferred_element_type=jnp.float32)  19.6 us
  transfers between devices with their start and end apart: 5, of which 4 were waited for; matrix products, arithmetic and copies ran while one was open for 13% of the time, Pallas kernels for 0%

profile of v1, /device:TPU:1, one launch (start us, length us, event | category | flops | bytes accessed | tf_op | source)
XLA Modules:
  0.0 505.2 jit_solution(9572615251793263686)
XLA Ops:
  8.0 0.0 reduce-scatter.5.cloned.1.call-start
  8.0 1.3 fusion.313
  10.1 0.0 copy-start.4
  10.1 11.9 %convolution_bitcast_fusion = f32[256,256]{1,0:T(8,128)} fusion(bf16[1,2,256,1792]{3,2,1,0:T(8,128)(2,1)} %param.6, s32[1792]{0:T(1024)S(1)} %fusion.205, s32[256]{0:T(256)S(1)} %and_select_fusion), kind=kOutput, calls=%fused_computation.211 | convolution fusion | flops 277544960 | bytes 1187840 | tf_op jit(solution)/shard_map/dot_general | solution.py:23
  22.1 0.0 reduce-scatter.5.cloned.1.call-update
  22.1 0.3 reduce-scatter.3.cloned.1.call-start
  23.1 0.0 copy-done.4
  23.1 0.0 copy-start.3
  23.1 10.6 %convolution_bitcast_fusion.1 = f32[256,256]{1,0:T(8,128)} fusion(bf16[1,2,256,1792]{3,2,1,0:T(8,128)(2,1)S(1)} %copy-done.4, s32[1792]{0:T(1024)S(1)} %fusion.191, s32[256]{0:T(256)S(1)} %and_select_fusion.2), kind=kOutput, calls=%fused_computation.212 | convolution fusion | flops 277544960 | bytes 1188864 | tf_op jit(solution)/shard_map/dot_general | solution.py:23
  33.7 0.0 reduce-scatter.3.cloned.1.call-update
  33.8 0.4 all-reduce.4.cloned.1.call-start
  34.2 0.0 copy-done.3
  34.2 0.6 fusion.312
  36.1 0.1 fusion.184
  36.3 20.4 %fusion.138 = f32[256,256]{1,0:T(8,128)} fusion(s32[1792]{0:T(1024)S(1)} %fusion.191, s32[256]{0:T(256)S(1)} %and_select_fusion.2, s32[1792]{0:T(1024)S(1)} %get-tuple-element.11, s32[256]{0:T(256)S(1)} %and_select_fusion.3), kind=kOutput, calls=%fused_computation.226 | convolution fusion | flops 320208896 | bytes 278528 | tf_op jit(solution)/shard_map/dot_general | solution.py:23
  56.7 0.0 copy-start.1
  56.7 0.0 copy-start.2
  56.7 0.0 copy-start.5
  56.7 20.8 %fusion.136 = f32[256,256]{1,0:T(8,128)} fusion(s32[1792]{0:T(1024)S(1)} %get-tuple-element.12, s32[256]{0:T(256)S(1)} %and_select_fusion.1, s32[1792]{0:T(1024)S(1)} %fusion.205, s32[256]{0:T(256)S(1)} %and_select_fusion), kind=kOutput, calls=%fused_computation.225 | convolution fusion | flops 320208896 | bytes 278528 | tf_op jit(solution)/shard_map/dot_general | solution.py:23
  77.5 0.0 all-reduce.4.cloned.1.call-update
  77.5 95.9 %reduce-scatter.5.cloned.1.call-done = f32[8,256]{1,0:T(8,128)} async-done(((f32[256,256]{1,0:T(8,128)}), f32[8,256]{1,0:T(8,128)}) %reduce-scatter.5.cloned.1.call-update) | async-done | bytes 8208 | tf_op jit(solution)/shard_map/reduce_scatter | solution.py:47
  173.5 149.9 %reduce-scatter.3.cloned.1.call-done = f32[8,256]{1,0:T(8,128)} async-done(((f32[256,256]{1,0:T(8,128)}), f32[8,256]{1,0:T(8,128)}) %reduce-scatter.3.cloned.1.call-update) | async-done | bytes 8208 | tf_op jit(solution)/shard_map/reduce_scatter | solution.py:47
  323.4 84.4 %all-reduce = (f32[8,256]{1,0:T(8,128)S(1)}, f32[8,256]{1,0:T(8,128)S(1)}) all-reduce(f32[8,256]{1,0:T(8,128)} %reduce-scatter.5.cloned.1.call-done, f32[8,256]{1,0:T(8,128)} %reduce-scatter.3.cloned.1.call-done), channel_id=1, replica_groups=mesh['dp'=32,'mp'=16] {'mp'}, use_global_device_ids=true, to_apply=%region_5.6 | all-reduce | flops 4096 | bytes 32768 | tf_op jit(solution)/shard_map/psum | solution.py:48
  407.8 0.0 all-reduce.4.cloned.1.call-done
  407.8 0.0 copy-done.1
  407.8 1.2 fusion.129
  408.9 0.0 copy-done.2
  409.0 1.2 fusion.131
  410.1 0.0 copy-done.5
  410.2 9.8 %fusion.3 = bf16[8,1792]{1,0:T(8,128)(2,1)S(1)} fusion(s32[1792]{0:T(1024)S(1)} %fusion.205, s32[256]{0:T(256)S(1)} %and_select_fusion, bf16[2,8,1792]{2,1,0:T(8,128)(2,1)S(1)} %copy-done.5, f32[8,256]{1,0:T(8,128)S(1)} %fusion.131, f32[8,256]{1,0:T(8,128)S(1)} %fusion.129), kind=kOutput, calls=%fused_computation.69 | convolution fusion | flops 50067456 | bytes 81920 | tf_op jit(solution)/shard_map/dot_general | solution.py:61
  420.0 0.0 copy-start
  420.0 1.0 stack.19
  421.0 21.1 %all-to-all-start.1 = ((bf16[32,8,1792]{2,1,0:T(8,128)(2,1)}), bf16[32,8,1792]{2,1,0:T(8,128)(2,1)S(1)}, u32[]{:S(2)}, u32[]{:S(2)}) async-start(bf16[32,8,1792]{2,1,0:T(8,128)(2,1)} %stack.19), calls=%async_computation.3 | async-start | bytes 1835008 | tf_op jit(solution)/shard_map/all_to_all | solution.py:65
  442.1 0.0 copy-done
  442.1 0.2 fusion.133
  442.3 0.3 fusion.135
  442.5 9.8 %fusion.2 = bf16[8,1792]{1,0:T(8,128)(2,1)S(1)} fusion(s32[1792]{0:T(1024)S(1)} %fusion.191, s32[256]{0:T(256)S(1)} %and_select_fusion.2, bf16[2,8,1792]{2,1,0:T(8,128)(2,1)S(1)} %copy-done.5, f32[8,256]{1,0:T(8,128)S(1)} %fusion.135, f32[8,256]{1,0:T(8,128)S(1)} %fusion.133), kind=kOutput, calls=%fused_computation.68 | convolution fusion | flops 50067456 | bytes 81920 | tf_op jit(solution)/shard_map/dot_general | solution.py:61
  452.4 13.7 %all-to-all-done.1 = bf16[32,8,1792]{2,1,0:T(8,128)(2,1)S(1)} async-done(((bf16[32,8,1792]{2,1,0:T(8,128)(2,1)}), bf16[32,8,1792]{2,1,0:T(8,128)(2,1)S(1)}, u32[]{:S(2)}, u32[]{:S(2)}) %all-to-all-start.1) | async-done | bytes 917536 | tf_op jit(solution)/shard_map/all_to_all | solution.py:65
  466.1 1.0 stack.18
  467.1 4.8 all-to-all-start
  471.9 0.6 pad_maximum_fusion.2
  472.5 0.6 pad_maximum_fusion.1
  473.1 22.8 %all-to-all-done = bf16[32,8,1792]{2,1,0:T(8,128)(2,1)S(1)} async-done(((bf16[32,8,1792]{2,1,0:T(8,128)(2,1)}), bf16[32,8,1792]{2,1,0:T(8,128)(2,1)S(1)}, u32[]{:S(2)}, u32[]{:S(2)}) %all-to-all-start) | async-done | bytes 917536 | tf_op jit(solution)/shard_map/all_to_all | solution.py:65
  496.0 1.4 pad_maximum_fusion
  (6 shorter events, 0.2 us)
Async XLA Ops:
  8.0 165.5 %reduce-scatter.5.cloned.1.call-start = ((), (), s32[]{:S(2)}) async-start(), calls=%async_computation.5 | async-start | bytes 270336 | tf_op jit(solution)/shard_map/reduce_scatter | solution.py:47
  10.1 13.0 %copy-start.4 = (bf16[1,2,256,1792]{3,2,1,0:T(8,128)(2,1)S(1)}, bf16[1,2,256,1792]{3,2,1,0:T(8,128)(2,1)}, u32[]{:S(2)}) copy-start(bf16[1,2,256,1792]{3,2,1,0:T(8,128)(2,1)} %param.6) | copy-start | bytes 5505028
  22.1 301.3 %reduce-scatter.3.cloned.1.call-start = ((), (), s32[]{:S(2)}) async-start(), calls=%async_computation.4 | async-start | bytes 270336 | tf_op jit(solution)/shard_map/reduce_scatter | solution.py:47
  23.1 11.1 %copy-start.3 = (s32[2]{0:T(128)S(1)}, s32[2]{0:T(128)}, u32[]{:S(2)}) copy-start(s32[2]{0:T(128)} %param.10) | copy-start | bytes 28
  33.8 374.0 %all-reduce.4.cloned.1.call-start = ((), (), s32[]{:S(2)}) async-start(), calls=%async_computation.6 | async-start | bytes 1048576 | tf_op jit(solution)/shard_map/psum | solution.py:45
  56.7 351.1 %copy-start.1 = (f32[2,8,256]{2,1,0:T(8,128)S(1)}, f32[2,8,256]{2,1,0:T(8,128)}, u32[]{:S(2)}) copy-start(f32[2,8,256]{2,1,0:T(8,128)} %param.9) | copy-start | bytes 49156
  56.7 352.3 %copy-start.2 = (f32[2,8,256]{2,1,0:T(8,128)S(1)}, f32[2,8,256]{2,1,0:T(8,128)}, u32[]{:S(2)}) copy-start(f32[2,8,256]{2,1,0:T(8,128)} %param.8) | copy-start | bytes 49156
  56.7 353.5 %copy-start.5 = (bf16[2,8,1792]{2,1,0:T(8,128)(2,1)S(1)}, bf16[2,8,1792]{2,1,0:T(8,128)(2,1)}, u32[]{:S(2)}) copy-start(bf16[2,8,1792]{2,1,0:T(8,128)(2,1)} %param.7) | copy-start | bytes 172036
  420.0 22.1 %copy-start = (f32[256,256]{1,0:T(8,128)S(1)}, f32[256,256]{1,0:T(8,128)}, u32[]{:S(2)}) copy-start(f32[256,256]{1,0:T(8,128)} %get-tuple-element.6) | copy-start | bytes 786436
  421.0 45.1 %all-to-all-start.1 = ((bf16[32,8,1792]{2,1,0:T(8,128)(2,1)}), bf16[32,8,1792]{2,1,0:T(8,128)(2,1)S(1)}, u32[]{:S(2)}, u32[]{:S(2)}) async-start(bf16[32,8,1792]{2,1,0:T(8,128)(2,1)} %stack.19), calls=%async_computation.3 | async-start | bytes 1835008 | tf_op jit(solution)/shard_map/all_to_all | solution.py:65
  467.1 28.9 %all-to-all-start = ((bf16[32,8,1792]{2,1,0:T(8,128)(2,1)}), bf16[32,8,1792]{2,1,0:T(8,128)(2,1)S(1)}, u32[]{:S(2)}, u32[]{:S(2)}) async-start(bf16[32,8,1792]{2,1,0:T(8,128)(2,1)} %stack.18), calls=%async_computation.1 | async-start | bytes 1835008 | tf_op jit(solution)/shard_map/all_to_all | solution.py:65
Sparse Core Ops, SparseCore 0:
  22.2 151.2 reduce-scatter.4
  176.2 147.0 reduce-scatter.2
Sparse Core Ops, SparseCore 1:
  77.6 199.4 all-reduce.3
